TPU v7x, 32 devices: a whole 2x2x4 slice. The times are simulated.
32 devices in a mesh: batch: 8 (over y, x, core), lib: 4 (over z).
Axes of the slice: x: 2, y: 2, z: 4, core: 2. Of those that a mesh axis runs over, the one named last changes fastest.
Arguments:
- skip_features: bfloat16 [64, 1024, 320], P(('batch', 'lib')), may hold values from -6 to 6
- cached_deep_features: bfloat16 [64, 1024, 640], P('lib', 'batch'), may hold values from -6 to 6
- target_position: int32 [4, 16], P('lib'), may hold values from 0 to 15, each once within a row
- request_adapter: int32 [64], P(('batch', 'lib')), may hold values from 0 to 15
- library_adapter: int32 [16], P('lib'), may hold values from 0 to 15, each once
- adapter_down_weight: bfloat16 [16, 64, 960], P('lib'), may hold values from -0.1875 to 0.1875
- adapter_up_weight: bfloat16 [16, 64, 320], P('lib'), may hold values from -0.75 to 0.75
- kernel_weight: bfloat16 [3, 3, 960, 320], replicated, may hold values from -0.0625 to 0.0625
- shortcut_matrix: bfloat16 [960, 320], replicated, may hold values from -0.1875 to 0.1875
- group_norm_gain: float32 [960], replicated, may hold values from 0.5 to 1.5
- group_norm_offset: float32 [960], replicated, may hold values from -1.8 to 1.8
- output_bias: float32 [320], replicated, may hold values from -1.8 to 1.8
Outputs:
- block_out: bfloat16 [64, 1024, 320], P(('batch', 'lib'))
Inputs may be any that keep to these rules, and one draw needn't show every extreme that they name: Each row of target_position names every one of its 16 slots once. `request_adapter`: ids of adapters in the library. `library_adapter`: every adapter id is held in exactly one library slot.
All inputs are finite; a program needn't handle non-finite values.
Results may differ from a plain program's by a relative error of at most 0.0045.
Values may be sent and summed in bfloat16 or wider, within the bound.
A program may use at most 128 MiB of HBM per device.

v0:
```python
import jax
import jax.numpy as jnp
from jax import lax
from jax.sharding import PartitionSpec as P

DEEP = 640
GROUPS = 32
ROWS = 32
LAT_W = 32


def norm_silu(joined, group_norm_gain, group_norm_offset):
    count = joined.shape[0]
    places = joined.shape[1]
    width = joined.shape[2]
    values = joined.astype(jnp.float32).reshape(count, places, GROUPS, width // GROUPS)
    center = jnp.mean(values, axis=(1, 3), keepdims=True)
    spread = jnp.mean((values - center) ** 2, axis=(1, 3), keepdims=True)
    scaled = ((values - center) / jnp.sqrt(spread + 1e-05)).reshape(
        count, places, width
    ) * group_norm_gain + group_norm_offset
    return jax.nn.silu(scaled).astype(jnp.bfloat16)


def local(
    skip_features,
    cached_deep_features,
    target_position,
    request_adapter,
    library_adapter,
    adapter_down_weight,
    adapter_up_weight,
    kernel_weight,
    shortcut_matrix,
    group_norm_gain,
    group_norm_offset,
    output_bias,
):
    batch_count = lax.axis_size("batch")
    per_device = skip_features.shape[0]
    places = skip_features.shape[1]
    column = target_position.shape[1]
    width = kernel_weight.shape[2]
    outputs = kernel_weight.shape[3]
    placing = target_position[0]
    inverse = jnp.zeros((column,), jnp.int32).at[placing].set(jnp.arange(column, dtype=jnp.int32))
    order = inverse.reshape(batch_count, per_device).T
    outgoing = cached_deep_features[order]
    arrived = lax.all_to_all(outgoing, "batch", split_axis=1, concat_axis=1, tiled=True)
    deep = arrived.reshape(per_device, places, DEEP)
    down_portion = lax.all_gather(adapter_down_weight, "lib", axis=0, tiled=True)
    up_portion = lax.all_gather(adapter_up_weight, "lib", axis=0, tiled=True)
    id_piece = lax.all_gather(library_adapter, "lib", axis=0, tiled=True)
    picker = (request_adapter[:, None] == id_piece[None, :]).astype(jnp.bfloat16)
    down_sum = jnp.einsum("rk,kij->rij", picker, down_portion, preferred_element_type=jnp.float32)
    up_sum = jnp.einsum("rk,kij->rij", picker, up_portion, preferred_element_type=jnp.float32)
    down_sum, up_sum = (down_sum, up_sum)
    down_blocks = down_sum.astype(jnp.bfloat16)
    up_blocks = up_sum.astype(jnp.bfloat16)
    joined = jnp.concatenate([skip_features, deep], axis=2)
    normed = norm_silu(joined, group_norm_gain, group_norm_offset)
    padded = jnp.pad(
        normed.reshape(per_device, ROWS, LAT_W, width), ((0, 0), (1, 1), (1, 1), (0, 0))
    )
    conv = jnp.zeros((per_device * places, outputs), jnp.float32)
    for row_off in range(3):
        for col_off in range(3):
            window = padded[:, row_off : row_off + ROWS, col_off : col_off + LAT_W].reshape(
                per_device * places, width
            )
            conv = conv + jnp.dot(
                window, kernel_weight[row_off, col_off], preferred_element_type=jnp.float32
            )
    shortcut = jnp.dot(
        joined.reshape(per_device * places, width),
        shortcut_matrix,
        preferred_element_type=jnp.float32,
    )
    low = jnp.einsum(
        "rpc,rkc->rpk", normed, down_blocks, preferred_element_type=jnp.float32
    ).astype(jnp.bfloat16)
    delta = jnp.einsum("rpk,rko->rpo", low, up_blocks, preferred_element_type=jnp.float32)
    total = (shortcut + conv).reshape(per_device, places, outputs) + output_bias + delta
    return total.astype(jnp.bfloat16)


def solution(mesh):
    in_specs = (
        P(("batch", "lib"), None, None),
        P("lib", "batch", None),
        P("lib", None),
        P(("batch", "lib")),
        P("lib"),
        P("lib", None, None),
        P("lib", None, None),
        P(),
        P(),
        P(),
        P(),
        P(),
    )
    out_specs = P(("batch", "lib"), None, None)
    return jax.shard_map(local, mesh=mesh, in_specs=in_specs, out_specs=out_specs, check_vma=False)
```

profile of v0, /device:TPU:0, one launch (start us, length us, event | category | flops | bytes accessed | tf_op | source)
XLA Modules:
  0.0 148.1 jit_solution(5434966734072437644)
XLA Ops:
  6.5 0.8 fusion.48
  7.3 0.6 scatter_custom_fusion
  8.0 0.1 reshape.168
  8.1 0.1 copy.33
  8.1 0.1 reshape.181
  8.2 0.1 copy-done
  8.3 2.4 %gather_fusion = bf16[16,128,640]{2,1,0:T(8,128)(2,1)} fusion(bf16[16,128,640]{2,1,0:T(8,128)(2,1)S(1)} %copy-done, s32[1024]{0:T(1024)S(1)} %pad_clamp_fusion), kind=kCustom, calls=%fused_computation | custom fusion | bytes 5242944 | tf_op jit(solution)/shard_map/gather | solution.py:48
  10.7 3.6 %copy.34 = bf16[2,8,128,640]{3,2,0,1:T(8,128)(2,1)} copy(bf16[2,8,128,640]{3,2,1,0:T(8,128)(2,1)} %bitcast.86) | data formatting | bytes 5242880 | tf_op jit(solution)/shard_map/gather | solution.py:48
  14.3 5.3 %all-to-all-start = ((bf16[2,8,128,640]{3,2,0,1:T(8,128)(2,1)}), bf16[2,8,128,640]{3,2,0,1:T(8,128)(2,1)}, u32[]{:S(2)}, u32[]{:S(2)}) async-start(bf16[2,8,128,640]{3,2,0,1:T(8,128)(2,1)} %copy.34), calls=%async_computation | async-start | bytes 5242880 | tf_op jit(solution)/shard_map/all_to_all | solution.py:49
  19.6 0.0 all-gather.2.cloned.1.call-start
  19.6 0.7 all-gather.2.cloned.1.call-update
  20.3 1.6 %copy.49 = bf16[2,1024,320]{2,1,0:T(8,128)(2,1)} copy(bf16[2,1024,320]{1,2,0:T(8,128)(2,1)S(1)} %copy-done.9) | data formatting | bytes 2621440 | tf_op jit(solution)/shard_map/concatenate | solution.py:60
  21.9 0.6 dynamic-slice
  23.2 0.2 dynamic-update-slice
  23.4 9.2 %all-reduce.1 = s32[16]{0:T(128)S(1)} all-reduce(s32[16]{0:T(128)S(1)} %dynamic-update-slice), channel_id=1, replica_groups=mesh['batch'=8,'lib'=4] {'lib'}, use_global_device_ids=true, to_apply=%add.1 | all-reduce | flops 16 | bytes 128
  32.6 29.5 %all_gather.11 = bf16[16,64,320]{2,1,0:T(8,128)(2,1)S(1)} all-gather(bf16[4,64,320]{2,1,0:T(8,128)(2,1)S(1)} %copy-done.10), channel_id=1, replica_groups=mesh['batch'=8,'lib'=4] {'lib'}, dimensions={0}, use_global_device_ids=true | all-gather | bytes 819200 | tf_op jit(solution)/shard_map/all_gather | solution.py:52
  62.1 0.5 convolution_convert_fusion.1
  62.7 2.2 %copy.35 = bf16[2,8,128,640]{3,2,1,0:T(8,128)(2,1)S(1)} copy(bf16[2,8,128,640]{3,2,0,1:T(8,128)(2,1)} %all-to-all-done) | data formatting | bytes 5242880 | tf_op jit(solution)/shard_map/all_to_all | solution.py:49
  64.9 1.7 %convert_reduce_fusion = f32[2,960]{1,0:T(2,128)S(1)} fusion(bf16[2,1024,640]{2,1,0:T(8,128)(2,1)S(1)} %bitcast.72, bf16[2,1024,320]{2,1,0:T(8,128)(2,1)S(1)} %copy-done.2), kind=kLoop, calls=%fused_computation.3 | loop fusion | flops 9828480 | bytes 3939840 | tf_op jit(solution)/shard_map/reduce_sum | solution.py:17
  66.7 0.1 reduce_sum.24
  66.8 0.1 reduce_sum.25
  66.9 0.1 sub.31
  66.9 0.1 sub.32
  67.1 3.6 %fusion.2 = f32[2,960]{1,0:T(2,128)S(1)} fusion(f32[2,960]{1,0:T(2,128)S(1)} %sub.32, bf16[2,1024,640]{2,1,0:T(8,128)(2,1)S(1)} %bitcast.73, bf16[2,1024,320]{2,1,0:T(8,128)(2,1)} %copy.49), kind=kLoop, calls=%fused_computation.6 | loop fusion | flops 13760640 | bytes 3947520 | tf_op jit(solution)/shard_map/reduce_sum | solution.py:18
  70.7 0.1 reduce_sum.36
  70.8 0.1 reduce_sum.37
  70.9 0.1 div.49
  70.9 0.1 div.50
  71.1 6.8 %multiply_convert_fusion = bf16[2,1024,960]{2,1,0:T(8,128)(2,1)} fusion(f32[960]{0:T(1024)S(1)} %copy-done.11, f32[960]{0:T(1024)S(1)} %copy-done.12, f32[2,960]{1,0:T(2,128)S(1)} %div.50, f32[2,960]{1,0:T(2,128)S(1)} %sub.32, bf16[2,1024,640]{2,1,0:T(8,128)(2,1)S(1)} %bitcast.74, bf16[2,1024,320]{2,1,0:T(8,128)(2,1)} %copy.49), kind=kLoop, calls=%fused_computation.9 | loop fusion | flops 25559040 | bytes 7887360 | tf_op jit(solution)/shard_map/convert_element_type | solution.py:22
  77.9 5.6 %multiply_convert_fusion.1 = bf16[2,32,32,960]{3,2,1,0:T(8,128)(2,1)} fusion(bf16[2,32,32,640]{3,2,1,0:T(8,128)(2,1)S(1)} %bitcast.75, bf16[2,32,32,320]{3,2,1,0:T(8,128)(2,1)S(1)} %bitcast.77, f32[960]{0:T(1024)S(1)} %copy-done.11, f32[960]{0:T(1024)S(1)} %copy-done.12, f32[2,960]{1,0:T(2,128)S(1)} %div.50, f32[2,960]{1,0:T(2,128)S(1)} %sub.32), kind=kLoop, calls=%fused_computation.10 | loop fusion | flops 25559040 | bytes 7887360 | tf_op jit(solution)/shard_map/convert_element_type | solution.py:22
  83.5 22.2 %pad_slice_fusion = (bf16[2,32,32,960]{3,2,1,0:T(8,128)(2,1)S(1)}, bf16[2,32,32,960]{3,2,1,0:T(8,128)(2,1)}, bf16[2,32,32,960]{3,2,1,0:T(8,128)(2,1)}, bf16[2,32...) fusion(bf16[2,32,32,960]{3,2,1,0:T(8,128)(2,1)} %multiply_conve, ...), kind=kLoop, calls=%fused_computation.11 | loop fusion | bytes 35389440 | tf_op jit(solution)/shard_map/slice | solution.py:68
  105.8 0.0 slice-start
  105.8 4.1 %fusion.30 = f32[2048,320]{0,1:T(8,128)S(1)} fusion(bf16[2048,960]{1,0:T(8,128)(2,1)} %bitcast.88, bf16[3,3,960,320]{2,3,1,0:T(8,128)(2,1)} %param.19), kind=kOutput, calls=%fused_computation.51 | convolution fusion | flops 1258291200 | bytes 7471104 | tf_op jit(solution)/shard_map/dot_general | solution.py:71
  109.9 0.0 slice-start.1
  109.9 2.8 %convolution_add_fusion.6 = f32[2048,320]{0,1:T(8,128)S(1)} fusion(f32[2048,320]{0,1:T(8,128)S(1)} %fusion.30, bf16[2048,960]{1,0:T(8,128)(2,1)S(1)} %bitcast.84, bf16[3,3,960,320]{2,3,1,0:T(8,128)(2,1)} %param.19), kind=kOutput, calls=%fused_computation.32 | convolution fusion | flops 1258946560 | bytes 9830400 | tf_op jit(solution)/shard_map/dot_general | solution.py:71
  112.7 0.2 slice-done.1
  112.9 1.6 %convolution_add_fusion.5 = f32[2048,320]{0,1:T(8,128)S(1)} fusion(f32[2048,320]{0,1:T(8,128)S(1)} %convolution_add_fusion.6, bf16[2048,960]{1,0:T(8,128)(2,1)S(1)} %bitcast.83, bf16[3,3,960,320]{2,3,1,0:T(8,128)(2,1)S(1)} %bitcast.90), kind=kOutput, calls=%fused_computation.31 | convolution fusion | flops 1258946560 | bytes 10092544 | tf_op jit(solution)/shard_map/dot_general | solution.py:71
  114.5 0.6 copy-done.4
  115.1 1.6 %convolution_add_fusion.4 = f32[2048,320]{0,1:T(8,128)S(1)} fusion(f32[2048,320]{0,1:T(8,128)S(1)} %convolution_add_fusion.5, bf16[2048,960]{1,0:T(8,128)(2,1)S(1)} %bitcast.82, bf16[3,3,960,320]{2,3,1,0:T(8,128)(2,1)S(1)} %bitcast.90), kind=kOutput, calls=%fused_computation.30 | convolution fusion | flops 1258946560 | bytes 10092544 | tf_op jit(solution)/shard_map/dot_general | solution.py:71
  116.7 0.6 copy-done.8
  117.3 3.1 %fusion.24 = f32[2048,320]{0,1:T(8,128)} fusion(bf16[2048,960]{1,0:T(8,128)(2,1)S(1)} %bitcast.87, bf16[3,3,960,320]{2,3,1,0:T(8,128)(2,1)S(1)} %bitcast.90), kind=kOutput, calls=%fused_computation.45 | convolution fusion | flops 1258291200 | bytes 7471104 | tf_op jit(solution)/shard_map/dot_general | solution.py:71
  120.4 3.5 %fusion.12 = f32[2048,320]{0,1:T(8,128)S(1)} fusion(f32[2048,320]{0,1:T(8,128)} %fusion.24, f32[2048,320]{0,1:T(8,128)S(1)} %convolution_add_fusion.4, bf16[2048,960]{1,0:T(8,128)(2,1)S(1)} %bitcast.85, bf16[3,3,960,320]{2,3,1,0:T(8,128)(2,1)S(1)} %bitcast.90), kind=kOutput, calls=%fused_computation.26 | convolution fusion | flops 1259601920 | bytes 12713984 | tf_op jit(solution)/shard_map/dot_general | solution.py:71
  123.9 1.6 %convolution_add_fusion.3 = f32[2048,320]{0,1:T(8,128)S(1)} fusion(f32[2048,320]{0,1:T(8,128)S(1)} %fusion.12, bf16[2048,960]{1,0:T(8,128)(2,1)S(1)} %bitcast.81, bf16[3,3,960,320]{2,3,1,0:T(8,128)(2,1)S(1)} %bitcast.90), kind=kOutput, calls=%fused_computation.29 | convolution fusion | flops 1258946560 | bytes 10092544 | tf_op jit(solution)/shard_map/dot_general | solution.py:71
  125.5 1.6 %convolution_add_fusion.2 = f32[2048,320]{0,1:T(8,128)S(1)} fusion(f32[2048,320]{0,1:T(8,128)S(1)} %convolution_add_fusion.3, bf16[2048,960]{1,0:T(8,128)(2,1)S(1)} %bitcast.80, bf16[3,3,960,320]{2,3,1,0:T(8,128)(2,1)S(1)} %bitcast.90), kind=kOutput, calls=%fused_computation.28 | convolution fusion | flops 1258946560 | bytes 10092544 | tf_op jit(solution)/shard_map/dot_general | solution.py:71
  127.2 1.9 %convolution_add_fusion.1 = f32[2048,320]{0,1:T(8,128)S(1)} fusion(f32[2048,320]{0,1:T(8,128)S(1)} %convolution_add_fusion.2, bf16[2048,960]{1,0:T(8,128)(2,1)S(1)} %bitcast.79, bf16[3,3,960,320]{2,3,1,0:T(8,128)(2,1)S(1)} %bitcast.90), kind=kOutput, calls=%fused_computation.27 | convolution fusion | flops 1258946560 | bytes 10092544 | tf_op jit(solution)/shard_map/dot_general | solution.py:71
  129.1 3.3 %fusion.9 = f32[2048,320]{0,1:T(8,128)} fusion(f32[2048,320]{0,1:T(8,128)S(1)} %convolution_add_fusion.1, bf16[960,320]{0,1:T(8,128)(2,1)S(1)} %copy-done.15, bf16[2048,640]{1,0:T(8,128)(2,1)S(1)} %bitcast.76, bf16[2048,320]{1,0:T(8,128)(2,1)S(1)} %bitcast.78), kind=kOutput, calls=%fused_computation.24 | convolution fusion | flops 1266810880 | bytes 9789440 | tf_op jit(solution)/shard_map/dot_general | solution.py:74
  132.4 2.9 %fusion.17 = bf16[2,64,960]{2,0,1:T(2,128)(2,1)S(1)} fusion(bf16[16,64,960]{2,1,0:T(8,128)(2,1)} %all-gather.2.cloned.1.call-done, s32[16]{0:T(128)S(1)} %all-reduce.1, s32[2]{0:T(128)S(1)} %copy-done.14), kind=kOutput, calls=%fused_computation.39 | convolution fusion | flops 4055072 | bytes 2211912 | tf_op jit(solution)/shard_map/rk,kij->rij/dot_general | solution.py:55
  135.3 6.0 %fusion.14 = bf16[2,1024,320]{1,2,0:T(8,128)(2,1)} fusion(f32[40,2,8,1024]{3,2,1,0:T(8,128)} %bitcast.91, f32[320]{0:T(512)S(1)} %copy-done.13, bf16[2,1024,960]{2,1,0:T(8,128)(2,1)} %multiply_convert_fusion, bf16[2,64,960]{2,0,1:T(2,128)(2,1)S(1)} %fusion.17, bf16[2,64,320]{2,0,1:T(2,128)(2,1)S(1)} %convolution_convert_fusion.1), kind=kOutput, calls=%fused_computation.35 | convolution fusion | flops 337641472 | bytes 8193280 | tf_op jit(solution)/shard_map/rpk,rko->rpo/dot_general | solution.py:82
  (43 shorter events, 0.1 us)
Async XLA Ops:
  6.5 1.8 %copy-start = (bf16[16,128,640]{2,1,0:T(8,128)(2,1)S(1)}, bf16[16,128,640]{2,1,0:T(8,128)(2,1)}, u32[]{:S(2)}) copy-start(bf16[16,128,640]{2,1,0:T(8,128)(2,1)} %param.13) | copy-start | bytes 7864324
  14.3 6.1 %copy-start.9 = (bf16[2,1024,320]{1,2,0:T(8,128)(2,1)S(1)}, bf16[2,1024,320]{1,2,0:T(8,128)(2,1)}, u32[]{:S(2)}) copy-start(bf16[2,1024,320]{1,2,0:T(8,128)(2,1)} %param.12) | copy-start | bytes 3932164
  14.3 7.7 %copy-start.17 = (u32[32]{0:T(128)S(1)}, u32[32]{0:T(128)}, u32[]{:S(2)}) copy-start(u32[32]{0:T(128)} %constant.27) | copy-start | bytes 388
  14.3 8.9 %copy-start.16 = (s32[4]{0:T(128)S(1)}, s32[4]{0:T(128)}, u32[]{:S(2)}) copy-start(s32[4]{0:T(128)} %param.16) | copy-start | bytes 52
  14.3 18.3 %copy-start.10 = (bf16[4,64,320]{2,1,0:T(8,128)(2,1)S(1)}, bf16[4,64,320]{2,1,0:T(8,128)(2,1)}, u32[]{:S(2)}) copy-start(bf16[4,64,320]{2,1,0:T(8,128)(2,1)} %param.18) | copy-start | bytes 491524
  14.3 47.8 %copy-start.14 = (s32[2]{0:T(128)S(1)}, s32[2]{0:T(128)}, u32[]{:S(2)}) copy-start(s32[2]{0:T(128)} %param.15) | copy-start | bytes 28
  14.3 48.4 %all-to-all-start = ((bf16[2,8,128,640]{3,2,0,1:T(8,128)(2,1)}), bf16[2,8,128,640]{3,2,0,1:T(8,128)(2,1)}, u32[]{:S(2)}, u32[]{:S(2)}) async-start(bf16[2,8,128,640]{3,2,0,1:T(8,128)(2,1)} %copy.34), calls=%async_computation | async-start | bytes 5242880 | tf_op jit(solution)/shard_map/all_to_all | solution.py:49
  19.6 112.8 %all-gather.2.cloned.1.call-start = ((), (), s32[]{:S(2)}) async-start(), calls=%async_computation.1 | async-start | bytes 2621440 | tf_op jit(solution)/shard_map/all_gather | solution.py:51
  62.7 2.2 %copy-start.2 = (bf16[2,1024,320]{2,1,0:T(8,128)(2,1)S(1)}, bf16[2,1024,320]{2,1,0:T(8,128)(2,1)}, u32[]{:S(2)}) copy-start(bf16[2,1024,320]{2,1,0:T(8,128)(2,1)} %copy.49) | copy-start | bytes 3932164
  64.9 6.2 %copy-start.11 = (f32[960]{0:T(1024)S(1)}, f32[960]{0:T(1024)}, u32[]{:S(2)}) copy-start(f32[960]{0:T(1024)} %param.22) | copy-start | bytes 11524
  64.9 6.2 %copy-start.12 = (f32[960]{0:T(1024)S(1)}, f32[960]{0:T(1024)}, u32[]{:S(2)}) copy-start(f32[960]{0:T(1024)} %param.21) | copy-start | bytes 11524
  71.1 6.9 %copy-start.3 = (bf16[2,1024,320]{2,1,0:T(8,128)(2,1)S(1)}, bf16[2,1024,320]{2,1,0:T(8,128)(2,1)}, u32[]{:S(2)}) copy-start(bf16[2,1024,320]{2,1,0:T(8,128)(2,1)} %copy.49) | copy-start | bytes 3932164
  105.8 4.1 %copy-start.6 = (bf16[2,32,32,960]{3,2,1,0:T(8,128)(2,1)S(1)}, bf16[2,32,32,960]{3,2,1,0:T(8,128)(2,1)}, u32[]{:S(2)}) copy-start(bf16[2,32,32,960]{3,2,1,0:T(8,128)(2,1)} %get-tuple-element.6) | copy-start | bytes 11796484
  105.8 6.9 %slice-start = ((s8[5898240]{0:T(1024)(128)(4,1)}), s8[4194304]{0:T(1024)(128)(4,1)S(1)}, s32[]{:S(2)}) async-start(s8[5898240]{0:T(1024)(128)(4,1)} %bitcast.89), calls=%async_computation.2 | async-start | bytes 8388608
  109.9 2.9 %copy-start.5 = (bf16[2,32,32,960]{3,2,1,0:T(8,128)(2,1)S(1)}, bf16[2,32,32,960]{3,2,1,0:T(8,128)(2,1)}, u32[]{:S(2)}) copy-start(bf16[2,32,32,960]{3,2,1,0:T(8,128)(2,1)} %get-tuple-element.7) | copy-start | bytes 11796484
  109.9 3.0 %slice-start.1 = ((s8[5898240]{0:T(1024)(128)(4,1)}), s8[1703936]{0:T(1024)(128)(4,1)S(1)}, s32[]{:S(2)}) async-start(s8[5898240]{0:T(1024)(128)(4,1)} %bitcast.89), calls=%async_computation.3 | async-start | bytes 3407872
  112.9 2.2 %copy-start.4 = (bf16[2,32,32,960]{3,2,1,0:T(8,128)(2,1)S(1)}, bf16[2,32,32,960]{3,2,1,0:T(8,128)(2,1)}, u32[]{:S(2)}) copy-start(bf16[2,32,32,960]{3,2,1,0:T(8,128)(2,1)} %get-tuple-element.8) | copy-start | bytes 11796484
  115.1 2.2 %copy-start.8 = (bf16[2,32,32,960]{3,2,1,0:T(8,128)(2,1)S(1)}, bf16[2,32,32,960]{3,2,1,0:T(8,128)(2,1)}, u32[]{:S(2)}) copy-start(bf16[2,32,32,960]{3,2,1,0:T(8,128)(2,1)} %get-tuple-element.9) | copy-start | bytes 11796484
  117.3 3.1 %copy-start.7 = (bf16[2,1024,960]{2,1,0:T(8,128)(2,1)S(1)}, bf16[2,1024,960]{2,1,0:T(8,128)(2,1)}, u32[]{:S(2)}) copy-start(bf16[2,1024,960]{2,1,0:T(8,128)(2,1)} %multiply_convert_fusion) | copy-start | bytes 11796484
  127.2 1.9 %copy-start.15 = (bf16[960,320]{0,1:T(8,128)(2,1)S(1)}, bf16[960,320]{0,1:T(8,128)(2,1)}, u32[]{:S(2)}) copy-start(bf16[960,320]{0,1:T(8,128)(2,1)} %param.20) | copy-start | bytes 1843204
  129.1 6.2 %copy-start.13 = (f32[320]{0:T(512)S(1)}, f32[320]{0:T(512)}, u32[]{:S(2)}) copy-start(f32[320]{0:T(512)} %param.23) | copy-start | bytes 3844
  135.3 6.0 %copy-start.1 = (bf16[16,128,640]{2,1,0:T(8,128)(2,1)S(1)}, bf16[16,128,640]{2,1,0:T(8,128)(2,1)}, u32[]{:S(2)}) copy-start(bf16[16,128,640]{2,1,0:T(8,128)(2,1)} %param.13) | copy-start | bytes 7864324
Sparse Core Ops, SparseCore 0:
  22.0 60.5 all-gather.1
where the time goes:
time: 149 us; the launch traced here: 148 us
  blocking collectives  38.7 us (26%)
  local copies, waits for them, and re-layouts  35.9 us (24%)
  matrix products  34.4 us (23%)
  other arithmetic  18.8 us (13%)
  between operations  14.4 us (10%)
  starting transfers between devices  5.35 us (4%)
    all_gather x1, blocking collectives, local(): up_portion = lax.all_gather(adapter_up_weight, 'lib', axis=0, tiled=True)  29.5 us
    slice x1, local copies, waits for them, and re-layouts, local(): padded[:, row_off:row_off + ROWS, col_off:col_off + LAT_W]  22.2 us
    dot_general x9, matrix products, local(): jnp.dot(window, kernel_weight[row_off, col_off], preferred_element_type=j...  21.7 us
    convert_element_type x2, other arithmetic, norm_silu(): return jax.nn.silu(scaled).astype(jnp.bfloat16)  12.4 us
    unnamed x1, blocking collectives  9.15 us
    dot_general x1, matrix products, local(): jnp.einsum('rpk,rko->rpo', low, up_blocks, preferred_element_type=jnp.flo...  5.97 us
    gather x2, local copies, waits for them, and re-layouts, local(): outgoing = cached_deep_features[order]  5.97 us
    all_to_all x1, starting transfers between devices, local(): lax.all_to_all(outgoing, 'batch', split_axis=1, concat_axis=1, tiled=True)  5.31 us
  transfers between devices with their start and end apart: 2, of which 0 were waited for; matrix products, arithmetic and copies ran while one was open for 48% of the time, Pallas kernels for 0%

commit v1 on v0

v1 whole, which is shorter than its diff:
```python
import functools
import jax
import jax.numpy as jnp
import numpy as np
from jax import lax
from jax.experimental import pallas as pl
from jax.experimental.pallas import tpu as pltpu
from jax.sharding import PartitionSpec as P

GROUPS = 32
LAT_W = 32
SKIP = 320
DEEP = 640
WIDTH = SKIP + DEEP
OUT = 320
MAIN = 256
REST = OUT - MAIN
RANK = 64
CHUNK = 256
MESH = pl.DeviceIdType.MESH
PERM = ((0, 0, 256), (256, SKIP, DEEP), (256 + DEEP, 256, REST))


def same_group():
    order = np.concatenate([np.arange(s, s + n) for _, s, n in PERM])
    ids = order // (WIDTH // GROUPS)
    return (ids[:, None] == ids[None, :]).astype(np.float32)


def flip(value, mask, count):
    out, bit = 0, 1
    while bit < count:
        mine = (value // bit) % 2
        out = out + bit * ((1 - mine) if mask & bit else mine)
        bit *= 2
    return out


def move_kernel(B, L, tp, req, lib, cached, down, up, deep, dsel, usel,
                send, ids, dall, uall, s_send, s_recv, z_send, z_recv, f_send, f_recv, l_sem):
    b, l = lax.axis_index("batch"), lax.axis_index("lib")
    column, block = cached.shape[0], cached.shape[1]
    per = deep.shape[0]
    n = down.shape[0]
    h = n // 2
    half = b % 2
    peers = [flip(b, d, B) for d in range(B - 1, 0, -1)]
    zpeers = [(l + d) % L for d in range(1, L)]
    sib = peers[-1]

    barrier = pltpu.get_barrier_semaphore()
    for p in peers:
        pl.semaphore_signal(barrier, inc=1, device_id=(p, l), device_id_type=MESH)
    for z in zpeers:
        pl.semaphore_signal(barrier, inc=1, device_id=(b, z), device_id_type=MESH)
    pl.semaphore_wait(barrier, len(peers) + len(zpeers))

    def to_peer(s, p, src):
        t = p * per + s
        return pltpu.make_async_remote_copy(
            src_ref=send.at[t], dst_ref=deep.at[s, pl.ds(pl.multiple_of(src * block, block), block)],
            send_sem=s_send.at[s, p], recv_sem=s_recv.at[s, src],
            device_id=(p, l), device_id_type=MESH)

    def gather(t):
        j = jnp.int32(0)
        for i in range(column):
            j = jnp.where(tp[0, i] == t, i, j)
        send[t] = cached[j]

    def z_copies(z, src):
        part = pl.ds(half * h, h)
        row = pl.ds(src * n + half * h, h)
        kw = dict(device_id=(b, z), device_id_type=MESH)
        return [
            pltpu.make_async_remote_copy(src_ref=ids.at[src], dst_ref=ids.at[src],
                                         send_sem=z_send.at[0, z], recv_sem=z_recv.at[0, src], **kw),
            pltpu.make_async_remote_copy(src_ref=down.at[part], dst_ref=dall.at[row],
                                         send_sem=z_send.at[1, z], recv_sem=z_recv.at[1, src], **kw),
            pltpu.make_async_remote_copy(src_ref=up.at[part], dst_ref=uall.at[row],
                                         send_sem=z_send.at[2, z], recv_sem=z_recv.at[2, src], **kw),
        ]

    def f_copies(src, side):
        row = pl.ds(src * n + side * h, h)
        kw = dict(device_id=(sib, l), device_id_type=MESH)
        return [
            pltpu.make_async_remote_copy(src_ref=dall.at[row], dst_ref=dall.at[row],
                                         send_sem=f_send.at[0, src], recv_sem=f_recv.at[0, src], **kw),
            pltpu.make_async_remote_copy(src_ref=uall.at[row], dst_ref=uall.at[row],
                                         send_sem=f_send.at[1, src], recv_sem=f_recv.at[1, src], **kw),
        ]

    row_id = lax.broadcasted_iota(jnp.int32, ids.shape[1:], 0)
    mine = jnp.full(ids.shape[1:], -1, jnp.int32)
    for i in range(n):
        mine = jnp.where(row_id == i, lib[i], mine)
    ids[l] = mine
    for z in zpeers:
        for c in z_copies(z, l):
            c.start()
    own_d = pltpu.make_async_copy(down, dall.at[pl.ds(l * n, n)], l_sem.at[0])
    own_u = pltpu.make_async_copy(up, uall.at[pl.ds(l * n, n)], l_sem.at[1])
    own_d.start()
    own_u.start()
    for s in range(per):
        for p in peers:
            gather(p * per + s)
            to_peer(s, p, b).start()
    locals_ = []
    for s in range(per):
        gather(b * per + s)
        c = pltpu.make_async_copy(
            send.at[b * per + s], deep.at[s, pl.ds(pl.multiple_of(b * block, block), block)], l_sem.at[2 + s])
        c.start()
        locals_.append(c)
    for z in zpeers:
        for c in z_copies(z, z):
            c.wait_recv()
        for c in f_copies(z, half):
            c.start()
    for z in zpeers:
        for c in f_copies(z, 1 - half):
            c.wait_recv()
    own_d.wait()
    own_u.wait()
    number = lax.broadcasted_iota(jnp.int32, ids.shape, 0) * n + lax.broadcasted_iota(jnp.int32, ids.shape, 1)
    for s in range(per):
        k = jnp.max(jnp.where(ids[...] == req[s], number, 0))
        dsel[s] = dall[k]
        usel[s] = uall[k]
    for z in zpeers:
        for c in z_copies(z, l):
            c.wait_send()
        for c in f_copies(z, half):
            c.wait_send()
    for c in locals_:
        c.wait()
    for s in range(per):
        for p in peers:
            to_peer(s, p, p).wait_recv()
            to_peer(s, p, b).wait_send()


def move(B, L, tp, req, lib, cached, down, up, per, places):
    n, column, block = down.shape[0], cached.shape[0], cached.shape[1]
    vm = pl.BlockSpec(memory_space=pltpu.VMEM)
    sm = pl.BlockSpec(memory_space=pltpu.SMEM)
    dma = pltpu.SemaphoreType.DMA
    return pl.pallas_call(
        functools.partial(move_kernel, B, L),
        out_shape=(
            jax.ShapeDtypeStruct((per, places, DEEP), jnp.bfloat16),
            jax.ShapeDtypeStruct((per, RANK, WIDTH), jnp.bfloat16),
            jax.ShapeDtypeStruct((per, RANK, OUT), jnp.bfloat16),
        ),
        in_specs=[sm, sm, sm, vm, vm, vm],
        out_specs=(pl.BlockSpec(memory_space=pl.ANY), vm, vm),
        scratch_shapes=[
            pltpu.VMEM((column, block, DEEP), jnp.bfloat16),
            pltpu.VMEM((L, 8 * ((n + 7) // 8), 128), jnp.int32),
            pltpu.VMEM((L * n, RANK, WIDTH), jnp.bfloat16),
            pltpu.VMEM((L * n, RANK, OUT), jnp.bfloat16),
            dma((per, B)), dma((per, B)), dma((3, L)), dma((3, L)), dma((2, L)), dma((2, L)), dma((2 + per,)),
        ],
        compiler_params=pltpu.CompilerParams(
            collective_id=0, has_side_effects=True, vmem_limit_bytes=40 * 1024 * 1024),
    )(tp, req, lib, cached, down, up)


def build_weights(kw, w):
    for dc in range(3):
        for dst, src, n in PERM:
            rows, at = slice(src, src + n), slice(dst, dst + n)
            for dr in range(3):
                w[dc, at, dr * MAIN:(dr + 1) * MAIN] = kw[dr, dc, rows, :MAIN]
            w[dc, at, 768:896] = jnp.concatenate([kw[0, dc, rows, MAIN:], kw[1, dc, rows, MAIN:]], axis=1)
            w[dc, at, 896:1024] = jnp.concatenate(
                [kw[2, dc, rows, MAIN:], jnp.zeros((n, RANK), jnp.bfloat16)], axis=1)


def permuted(ref):
    return jnp.concatenate([ref[:, s:s + n] for _, s, n in PERM], axis=1)


def group_sum(v, same):
    v = jnp.sum(v, axis=0, keepdims=True)
    hi = v.astype(jnp.bfloat16).astype(jnp.float32)
    mid = (v - hi).astype(jnp.bfloat16).astype(jnp.float32)
    lo = v - hi - mid
    r = lax.broadcasted_iota(jnp.int32, (16, v.shape[1]), 0)
    rows = jnp.where(r == 0, hi, jnp.where(r == 1, mid, jnp.where(r == 2, lo, 0.0))).astype(jnp.bfloat16)
    return jnp.sum(jnp.dot(rows, same, preferred_element_type=jnp.float32), axis=0, keepdims=True)


def load_joined(skip, deep, at):
    sk = skip[0, at, :].astype(jnp.float32)
    return jnp.concatenate([sk[:, :256], deep[0, at, :].astype(jnp.float32), sk[:, 256:]], axis=1)


def block_kernel(skip, deep, dsel, usel, kw, sc, gain, offset, bias, same, out, w, x, acc):
    places = skip.shape[1]
    count = places * (WIDTH // GROUPS)

    @pl.when(pl.program_id(0) == 0)
    def _():
        build_weights(kw, w)

    dt = dsel[0].astype(jnp.float32).T.astype(jnp.bfloat16)
    for dst, src, n in PERM:
        w[1, dst:dst + n, 896:1024] = jnp.concatenate([kw[2, 1, src:src + n, MAIN:], dt[src:src + n]], axis=1)

    step = 64

    def total(i, c):
        v = load_joined(skip, deep, pl.ds(pl.multiple_of(i * step, step), step))
        return c + jnp.sum(v.reshape(step // 8, 8, WIDTH), axis=0)

    zero = jnp.zeros((8, WIDTH), jnp.float32)
    mean = group_sum(lax.fori_loop(0, places // step, total, zero), same[...]) * (1.0 / count)

    def square(i, c):
        v = load_joined(skip, deep, pl.ds(pl.multiple_of(i * step, step), step)) - mean
        return c + jnp.sum((v * v).reshape(step // 8, 8, WIDTH), axis=0)

    var = group_sum(lax.fori_loop(0, places // step, square, zero), same[...]) * (1.0 / count)
    scale = 0.5 * permuted(gain) * lax.rsqrt(var + 1e-5)
    shift = 0.5 * permuted(offset)

    def normed(i, c):
        at = pl.ds(pl.multiple_of(i * step, step), step)
        z = (load_joined(skip, deep, at) - mean) * scale + shift
        x[at, :] = (z + z * jnp.tanh(z)).astype(jnp.bfloat16)
        return c

    lax.fori_loop(0, places // step, normed, 0)

    def shortcut(i, c):
        p = pl.multiple_of(i * CHUNK, CHUNK)
        at = pl.ds(p, CHUNK)
        acc[pl.ds(p + LAT_W, CHUNK), :] = (
            jnp.dot(skip[0, at, :], sc[:SKIP, :], preferred_element_type=jnp.float32)
            + jnp.dot(deep[0, at, :], sc[SKIP:, :], preferred_element_type=jnp.float32)
            + bias[...]
        )
        return c

    lax.fori_loop(0, places // CHUNK, shortcut, 0)
    edge = jnp.zeros((LAT_W, OUT), jnp.float32)
    acc[:LAT_W, :] = edge
    acc[places + LAT_W:, :] = edge

    def conv(i, c):
        p = pl.multiple_of(i * CHUNK, CHUNK)
        xs = x[pl.ds(p, CHUNK), :]
        col = lax.broadcasted_iota(jnp.int32, (CHUNK, 1), 0) % LAT_W
        y1 = jnp.dot(xs, w[1], preferred_element_type=jnp.float32)
        y0 = jnp.dot(xs, w[0], preferred_element_type=jnp.float32)
        v = y1 + jnp.where(col != 0, pltpu.roll(y0, 1, 0), 0.0)
        y2 = jnp.dot(xs, w[2], preferred_element_type=jnp.float32)
        v = v + jnp.where(col != LAT_W - 1, pltpu.roll(y2, CHUNK - 1, 0), 0.0)
        low = y1[:, 3 * OUT:].astype(jnp.bfloat16)
        delta = jnp.dot(low, usel[0], preferred_element_type=jnp.float32)
        for dr in range(3):
            at = pl.ds(pl.multiple_of(p + (2 - dr) * LAT_W, LAT_W), CHUNK)
            a = v[:, dr * MAIN:(dr + 1) * MAIN]
            e = v[:, 3 * MAIN + dr * REST:3 * MAIN + (dr + 1) * REST]
            if dr == 1:
                a, e = a + delta[:, :MAIN], e + delta[:, MAIN:]
            acc[at, :MAIN] += a
            acc[at, MAIN:] += e
        return c

    lax.fori_loop(0, places // CHUNK, conv, 0)
    out[0] = acc[pl.ds(LAT_W, places), :].astype(jnp.bfloat16)


def compute(skip, deep, dsel, usel, kw, sc, gain, offset, bias):
    per, places = skip.shape[0], skip.shape[1]
    same = jnp.asarray(same_group(), jnp.bfloat16)
    vm = pl.BlockSpec(memory_space=pltpu.VMEM)

    def one(a):
        return pl.BlockSpec((1,) + a.shape[1:], lambda r: (r, 0, 0))

    return pl.pallas_call(
        block_kernel,
        grid=(per,),
        out_shape=jax.ShapeDtypeStruct((per, places, OUT), jnp.bfloat16),
        in_specs=[one(skip), one(deep), one(dsel), one(usel), vm, vm, vm, vm, vm, vm],
        out_specs=pl.BlockSpec((1, places, OUT), lambda r: (r, 0, 0)),
        scratch_shapes=[
            pltpu.VMEM((3, WIDTH, 1024), jnp.bfloat16),
            pltpu.VMEM((places, WIDTH), jnp.bfloat16),
            pltpu.VMEM((places + 2 * LAT_W, OUT), jnp.float32),
        ],
        compiler_params=pltpu.CompilerParams(vmem_limit_bytes=56 * 1024 * 1024),
    )(skip, deep, dsel, usel, kw, sc, gain[None], offset[None], bias[None], same)


def solution(mesh):
    B, L = mesh.shape["batch"], mesh.shape["lib"]

    def local(skip, cached, tp, req, lib, down, up, kw, sc, gain, offset, bias):
        per, places = skip.shape[0], skip.shape[1]
        deep, dsel, usel = move(B, L, tp, req, lib, cached, down, up, per, places)
        return compute(skip, deep, dsel, usel, kw, sc, gain, offset, bias)

    both = P(("batch", "lib"), None, None)
    lib3 = P("lib", None, None)
    in_specs = (both, P("lib", "batch", None), P("lib", None), P(("batch", "lib")), P("lib"), lib3, lib3,
                P(), P(), P(), P(), P())
    return jax.shard_map(local, mesh=mesh, in_specs=in_specs, out_specs=both, check_vma=False)
```

time: 149 us -> 96.3 us (0.65)
  the two profiles are of different devices: /device:TPU:0 before, /device:TPU:9 now
where the time goes in v1:
time: 96.3 us; the launch traced here: 95.9 us
  Pallas kernels  75 us (78%)
  local copies, waits for them, and re-layouts  20.9 us (22%)
    pallas_call x1, Pallas kernels, move(): pl.pallas_call(functools.partial(move_kernel, B, L), out_shape=(jax.Shape...  40.8 us
    pallas_call x1, Pallas kernels, compute(): pl.pallas_call(block_kernel, grid=(per,), out_shape=jax.ShapeDtypeStruct(...  34.2 us
    unnamed x21, local copies, waits for them, and re-layouts  17.1 us
    pallas_call x1, local copies, waits for them, and re-layouts, compute(): pl.pallas_call(block_kernel, grid=(per,), out_shape=jax.ShapeDtypeStruct(...  2.5 us

profile of v1, /device:TPU:9, one launch (start us, length us, event | category | flops | bytes accessed | tf_op | source)
XLA Modules:
  0.0 95.9 jit_solution(3085351255210095536)
XLA Ops:
  0.0 1.3 %broadcast_in_dim.11.bias = f32[1,320]{1,0:T(1,128)} reshape(f32[320]{0:T(512)} %param.24) | data formatting | bytes 2560 | tf_op jit(solution)/shard_map/broadcast_in_dim | solution.py:298
  1.3 0.0 copy-start
  1.3 0.0 copy-start.2
  1.3 0.0 copy-start.4
  1.3 0.0 copy-start.6
  1.3 0.0 copy-start.7
  1.3 0.0 copy-start.8
  1.3 2.4 %copy.16.sc = bf16[960,320]{1,0:T(8,128)(2,1)} copy(bf16[960,320]{0,1:T(8,128)(2,1)} %param.21) | data formatting | bytes 1228800 | tf_op args[8]
  3.7 2.6 %copy.14.skip = bf16[2,1024,320]{2,1,0:T(8,128)(2,1)} copy(bf16[2,1024,320]{1,2,0:T(8,128)(2,1)} %param.13) | data formatting | bytes 2621440 | tf_op args[0]
  6.3 0.0 copy-done
  6.3 0.0 copy-done.2
  6.3 0.0 copy-done.4
  6.3 0.0 copy-done.6
  6.3 0.0 copy-done.7
  6.3 0.0 copy-done.8
  6.3 40.8 %shard_map.127 = (bf16[2,1024,640]{2,1,0:T(8,128)(2,1)S(1)}, bf16[2,64,960]{2,1,0:T(8,128)(2,1)S(1)}, bf16[2,64,320]{2,1,0:T(8,128)(2,1)S(1)}) custom-call(s32[1,16]{1,0:T(1,128)S(1)} %copy-done.6, s32[2]{0:T(128)S(1)} %copy-done.7, s32[4]{0:T(128)S(1)} %copy-done.8, bf16[16,128,640]{2,1,0:T(8,128)(2,1)S(1)} %copy-done, bf16[4,64,960]{2,1,0:T(8,128)(2,1)S(1)} %copy-done.2, ...), custom_call_target="tpu_custom_call" | custom-call | tf_op jit(solution)/shard_map/pallas_call | solution.py:150
  47.1 0.0 copy-start.1
  47.1 1.5 %copy-done.1 = bf16[2,1024,640]{2,1,0:T(8,128)(2,1)} copy-done((bf16[2,1024,640]{2,1,0:T(8,128)(2,1)}, bf16[2,1024,640]{2,1,0:T(8,128)(2,1)S(1)}, u32[]{:S(2)}) %copy-start.1) | copy-done | bytes 2621464
  48.6 0.0 copy-start.3
  48.6 0.7 copy-done.3
  49.3 0.0 copy-start.5
  49.3 0.6 copy-done.5
  50.0 9.2 %copy.15.kw = bf16[3,3,960,320]{3,2,1,0:T(8,128)(2,1)} copy(bf16[3,3,960,320]{2,3,1,0:T(8,128)(2,1)} %param.20) | data formatting | bytes 11059200 | tf_op args[7]
  59.2 34.2 %shard_map.128 = bf16[2,1024,320]{2,1,0:T(8,128)(2,1)} custom-call(bf16[2,1024,320]{2,1,0:T(8,128)(2,1)} %copy.14.skip, bf16[2,1024,640]{2,1,0:T(8,128)(2,1)} %copy-done.1, bf16[2,64,960]{2,1,0:T(8,128)(2,1)} %copy-done.3, bf16[2,64,320]{2,1,0:T(8,128)(2,1)} %copy-done.5, bf16[3,3,960,320]{3,2,1,0:T(8,128)(2,1)} %copy.15.kw, bf16[960,320]{1,0:T(8,128)(2,1)} %copy.16.sc, ...), custom_call_target="tpu_custom_call" | custom-call | tf_op jit(solution)/shard_map/pallas_call | solution.py:286
  93.4 2.5 %copy.17 = bf16[2,1024,320]{1,2,0:T(8,128)(2,1)} copy(bf16[2,1024,320]{2,1,0:T(8,128)(2,1)} %shard_map.128) | data formatting | bytes 2621440 | tf_op jit(solution)/shard_map/pallas_call | solution.py:286
Async XLA Ops:
  1.3 5.0 %copy-start = (bf16[16,128,640]{2,1,0:T(8,128)(2,1)S(1)}, bf16[16,128,640]{2,1,0:T(8,128)(2,1)}, u32[]{:S(2)}) copy-start(bf16[16,128,640]{2,1,0:T(8,128)(2,1)} %cached.1) | copy-start | bytes 7864324
  1.3 5.0 %copy-start.2 = (bf16[4,64,960]{2,1,0:T(8,128)(2,1)S(1)}, bf16[4,64,960]{2,1,0:T(8,128)(2,1)}, u32[]{:S(2)}) copy-start(bf16[4,64,960]{2,1,0:T(8,128)(2,1)} %down.1) | copy-start | bytes 1474564
  1.3 5.0 %copy-start.4 = (bf16[4,64,320]{2,1,0:T(8,128)(2,1)S(1)}, bf16[4,64,320]{2,1,0:T(8,128)(2,1)}, u32[]{:S(2)}) copy-start(bf16[4,64,320]{2,1,0:T(8,128)(2,1)} %up.1) | copy-start | bytes 491524
  1.3 5.0 %copy-start.6 = (s32[1,16]{1,0:T(1,128)S(1)}, s32[1,16]{1,0:T(1,128)}, u32[]{:S(2)}) copy-start(s32[1,16]{1,0:T(1,128)} %tp.1) | copy-start | bytes 196
  1.3 5.0 %copy-start.7 = (s32[2]{0:T(128)S(1)}, s32[2]{0:T(128)}, u32[]{:S(2)}) copy-start(s32[2]{0:T(128)} %req.1) | copy-start | bytes 28
  1.3 5.0 %copy-start.8 = (s32[4]{0:T(128)S(1)}, s32[4]{0:T(128)}, u32[]{:S(2)}) copy-start(s32[4]{0:T(128)} %lib.1) | copy-start | bytes 52
  47.1 1.5 %copy-start.1 = (bf16[2,1024,640]{2,1,0:T(8,128)(2,1)}, bf16[2,1024,640]{2,1,0:T(8,128)(2,1)S(1)}, u32[]{:S(2)}) copy-start(bf16[2,1024,640]{2,1,0:T(8,128)(2,1)S(1)} %get-tuple-element.8.deep) | copy-start | bytes 7864324
  48.6 0.7 copy-start.3
  49.3 0.6 copy-start.5

commit v2 on v1

v2 whole, which is shorter than its diff:
```python
import functools
import jax
import jax.numpy as jnp
import numpy as np
from jax import lax
from jax.experimental import pallas as pl
from jax.experimental.pallas import tpu as pltpu
from jax.sharding import PartitionSpec as P

GROUPS = 32
LAT_W = 32
SKIP = 320
DEEP = 640
WIDTH = SKIP + DEEP
OUT = 320
MAIN = 256
REST = OUT - MAIN
RANK = 64
CHUNK = 256
MESH = pl.DeviceIdType.MESH
def same_group():
    ids = np.arange(WIDTH) // (WIDTH // GROUPS)
    return (ids[:, None] == ids[None, :]).astype(np.float32)


def dot_t(a, b):
    return lax.dot_general(a, b, (((1,), (1,)), ((), ())), preferred_element_type=jnp.float32)


def flip(value, mask, count):
    out, bit = 0, 1
    while bit < count:
        mine = (value // bit) % 2
        out = out + bit * ((1 - mine) if mask & bit else mine)
        bit *= 2
    return out


def group_sum(v, same):
    v = jnp.sum(v, axis=0, keepdims=True)
    hi = v.astype(jnp.bfloat16).astype(jnp.float32)
    mid = (v - hi).astype(jnp.bfloat16).astype(jnp.float32)
    lo = v - hi - mid
    r = lax.broadcasted_iota(jnp.int32, (16, v.shape[1]), 0)
    rows = jnp.where(r == 0, hi, jnp.where(r == 1, mid, jnp.where(r == 2, lo, 0.0))).astype(jnp.bfloat16)
    return jnp.sum(jnp.dot(rows, same, preferred_element_type=jnp.float32), axis=0, keepdims=True)


def kernel(B, L, tp, req, lib, cached_h, down, up, skip_h, kw_h, sc_h, gain, offset, bias, same_h, out,
           cached, send, deep, ids, dall, uall, w, sc, skip_t, skip, x, y, acc, same,
           s_send, s_recv, z_send, z_recv, f_send, f_recv, l_sem, w_sem):
    b, l = lax.axis_index("batch"), lax.axis_index("lib")
    column, block = cached.shape[0], cached.shape[1]
    per, places = deep.shape[0], deep.shape[1]
    n = down.shape[0]
    h = n // 2
    half = b % 2
    peers = [flip(b, d, B) for d in range(B - 1, 0, -1)]
    zpeers = [(l + d) % L for d in range(1, L)]
    sib = peers[-1]

    load_cached = pltpu.make_async_copy(cached_h, cached, l_sem.at[0])
    load_cached.start()
    loads = [
        pltpu.make_async_copy(skip_h, skip_t, l_sem.at[1]),
        pltpu.make_async_copy(sc_h, sc, l_sem.at[2]),
        pltpu.make_async_copy(same_h, same, l_sem.at[3]),
    ]
    w_loads = []
    for dr in range(3):
        for dc in range(3):
            i = 2 * (3 * dr + dc)
            w_loads.append(pltpu.make_async_copy(
                kw_h.at[dr, dc, pl.ds(0, MAIN)], w.at[dc, pl.ds(dr * MAIN, MAIN)], w_sem.at[i]))
            w_loads.append(pltpu.make_async_copy(
                kw_h.at[dr, dc, pl.ds(MAIN, REST)], w.at[dc, pl.ds(3 * MAIN + dr * REST, REST)], w_sem.at[i + 1]))

    barrier = pltpu.get_barrier_semaphore()
    for p in peers:
        pl.semaphore_signal(barrier, inc=1, device_id=(p, l), device_id_type=MESH)
    for z in zpeers:
        pl.semaphore_signal(barrier, inc=1, device_id=(b, z), device_id_type=MESH)
    pl.semaphore_wait(barrier, len(peers) + len(zpeers))

    def to_peer(s, p, src):
        return pltpu.make_async_remote_copy(
            src_ref=send.at[p * per + s], dst_ref=deep.at[s, pl.ds(pl.multiple_of(src * block, block), block)],
            send_sem=s_send.at[s, p], recv_sem=s_recv.at[s, src],
            device_id=(p, l), device_id_type=MESH)

    def slot(t):
        j = jnp.int32(0)
        for i in range(column):
            j = jnp.where(tp[0, i] == t, i, j)
        return j

    def z_copies(z, src):
        part = pl.ds(half * h, h)
        row = pl.ds(src * n + half * h, h)
        kw = dict(device_id=(b, z), device_id_type=MESH)
        return [
            pltpu.make_async_remote_copy(src_ref=ids.at[src], dst_ref=ids.at[src],
                                         send_sem=z_send.at[0, z], recv_sem=z_recv.at[0, src], **kw),
            pltpu.make_async_remote_copy(src_ref=down.at[part], dst_ref=dall.at[row],
                                         send_sem=z_send.at[1, z], recv_sem=z_recv.at[1, src], **kw),
            pltpu.make_async_remote_copy(src_ref=up.at[part], dst_ref=uall.at[row],
                                         send_sem=z_send.at[2, z], recv_sem=z_recv.at[2, src], **kw),
        ]

    def f_copies(src, side):
        row = pl.ds(src * n + side * h, h)
        kw = dict(device_id=(sib, l), device_id_type=MESH)
        return [
            pltpu.make_async_remote_copy(src_ref=dall.at[row], dst_ref=dall.at[row],
                                         send_sem=f_send.at[0, src], recv_sem=f_recv.at[0, src], **kw),
            pltpu.make_async_remote_copy(src_ref=uall.at[row], dst_ref=uall.at[row],
                                         send_sem=f_send.at[1, src], recv_sem=f_recv.at[1, src], **kw),
        ]

    load_cached.wait()
    for s in range(per):
        for p in peers:
            send[p * per + s] = cached[slot(p * per + s)]
            to_peer(s, p, b).start()
        if s == 0:
            row_id = lax.broadcasted_iota(jnp.int32, ids.shape[1:], 0)
            mine = jnp.full(ids.shape[1:], -1, jnp.int32)
            for i in range(n):
                mine = jnp.where(row_id == i, lib[i], mine)
            ids[l] = mine
            for z in zpeers:
                for c in z_copies(z, l):
                    c.start()
    for c in loads + w_loads:
        c.start()
    for s in range(per):
        deep[s, pl.ds(pl.multiple_of(b * block, block), block), :] = cached[slot(b * per + s)]
    dall[pl.ds(l * n, n)] = down[...]
    uall[pl.ds(l * n, n)] = up[...]
    edge = jnp.zeros((3, LAT_W, 1024), jnp.float32)
    y[:, :LAT_W, :] = edge
    y[:, places + LAT_W:, :] = edge
    for c in loads:
        c.wait()

    for s in range(per):
        for i in range(places // CHUNK):
            at = pl.ds(i * CHUNK, CHUNK)
            sk = skip_t[s, :, at].astype(jnp.float32).T.astype(jnp.bfloat16)
            skip[s, at, :] = sk
            acc[s, at, :] = dot_t(sk, sc[:, :SKIP]) + bias[...]

    for z in zpeers:
        for c in z_copies(z, z):
            c.wait_recv()
        for c in f_copies(z, half):
            c.start()
    for z in zpeers:
        for c in f_copies(z, 1 - half):
            c.wait_recv()
    for c in w_loads:
        c.wait()
    number = lax.broadcasted_iota(jnp.int32, ids.shape, 0) * n + lax.broadcasted_iota(jnp.int32, ids.shape, 1)
    count = places * (WIDTH // GROUPS)
    step = 64

    def request(s, carry):
        k = jnp.max(jnp.where(ids[...] == req[s], number, 0))
        w[1, 3 * OUT:, :] = dall[k]
        u = uall[k]
        for p in peers:
            to_peer(s, p, p).wait_recv()

        def both(i):
            at = pl.ds(pl.multiple_of(i * step, step), step)
            return skip[s, at, :].astype(jnp.float32), deep[s, at, :].astype(jnp.float32)

        def fold(v):
            return jnp.sum(v.reshape(step // 8, 8, v.shape[1]), axis=0)

        def total(i, c):
            a, d = both(i)
            return c[0] + fold(a), c[1] + fold(d)

        zero = (jnp.zeros((8, SKIP), jnp.float32), jnp.zeros((8, DEEP), jnp.float32))
        t = lax.fori_loop(0, places // step, total, zero)
        mean = group_sum(jnp.concatenate(t, axis=1), same[...]) * (1.0 / count)
        mean_s, mean_d = mean[:, :SKIP], mean[:, SKIP:]

        def square(i, c):
            a, d = both(i)
            a, d = a - mean_s, d - mean_d
            return c[0] + fold(a * a), c[1] + fold(d * d)

        t = lax.fori_loop(0, places // step, square, zero)
        var = group_sum(jnp.concatenate(t, axis=1), same[...]) * (1.0 / count)
        scale = 0.5 * gain[...] * lax.rsqrt(var + 1e-5)
        shift = 0.5 * offset[...]
        scale_s, scale_d = scale[:, :SKIP], scale[:, SKIP:]
        shift_s, shift_d = shift[:, :SKIP], shift[:, SKIP:]

        def normed(i, c):
            a, d = both(i)
            a = (a - mean_s) * scale_s + shift_s
            d = (d - mean_d) * scale_d + shift_d
            a = (a + a * jnp.tanh(a)).astype(jnp.bfloat16)
            d = (d + d * jnp.tanh(d)).astype(jnp.bfloat16)
            x[pl.ds(pl.multiple_of(i * step, step), step), :] = jnp.concatenate([a, d], axis=1)
            return c

        lax.fori_loop(0, places // step, normed, 0)

        def conv(i, c):
            p = pl.multiple_of(i * CHUNK, CHUNK)
            at = pl.ds(p, CHUNK)
            xs = x[at, :]
            to = pl.ds(pl.multiple_of(p + LAT_W, LAT_W), CHUNK)
            y1 = dot_t(xs, w[1])
            y[1, to, :] = y1
            y[0, to, :3 * OUT] = dot_t(xs, w[0, :3 * OUT])
            y[2, to, :3 * OUT] = dot_t(xs, w[2, :3 * OUT])
            acc[s, at, :] += (
                dot_t(deep[s, at, :], sc[:, SKIP:])
                + jnp.dot(y1[:, 3 * OUT:].astype(jnp.bfloat16), u, preferred_element_type=jnp.float32)
            )
            return c

        lax.fori_loop(0, places // CHUNK, conv, 0)
        side = 128

        def gather_taps(i, c):
            p = pl.multiple_of(i * side, side)
            col = lax.broadcasted_iota(jnp.int32, (side, 1), 0) % LAT_W

            def rows(dc, dr, lo, size):
                return y[dc, pl.ds(pl.multiple_of(p + dr * LAT_W, LAT_W), side), lo:lo + size]

            def column_sum(dc):
                a = rows(dc, 0, 0, MAIN) + rows(dc, 1, MAIN, MAIN) + rows(dc, 2, 2 * MAIN, MAIN)
                e = (rows(dc, 0, 3 * MAIN, 128) + rows(dc, 2, 3 * MAIN + 128, 128))[:, :REST]
                e = e + rows(dc, 1, 3 * MAIN, 128)[:, REST:]
                return jnp.concatenate([a, e], axis=1)

            v = column_sum(1) + acc[s, pl.ds(p, side), :]
            v = v + jnp.where(col != 0, pltpu.roll(column_sum(0), 1, 0), 0.0)
            v = v + jnp.where(col != LAT_W - 1, pltpu.roll(column_sum(2), side - 1, 0), 0.0)
            out[s, :, pl.ds(p, side)] = v.T.astype(jnp.bfloat16)
            return c

        lax.fori_loop(0, places // side, gather_taps, 0)
        return carry

    lax.fori_loop(0, per, request, 0)
    for z in zpeers:
        for c in z_copies(z, l):
            c.wait_send()
        for c in f_copies(z, half):
            c.wait_send()
    for s in range(per):
        for p in peers:
            to_peer(s, p, b).wait_send()


def solution(mesh):
    B, L = mesh.shape["batch"], mesh.shape["lib"]

    def local(skip, cached, tp, req, lib, down, up, kw, sc, gain, offset, bias):
        per, places = skip.shape[0], skip.shape[1]
        n, column, block = down.shape[0], cached.shape[0], cached.shape[1]
        vm = pl.BlockSpec(memory_space=pltpu.VMEM)
        sm = pl.BlockSpec(memory_space=pltpu.SMEM)
        hbm = pl.BlockSpec(memory_space=pl.ANY)
        dma = pltpu.SemaphoreType.DMA
        bf, f32 = jnp.bfloat16, jnp.float32
        out = pl.pallas_call(
            functools.partial(kernel, B, L),
            out_shape=jax.ShapeDtypeStruct((per, OUT, places), bf),
            in_specs=[sm, sm, sm, hbm, vm, vm, hbm, hbm, hbm, vm, vm, vm, hbm],
            out_specs=vm,
            scratch_shapes=[
                pltpu.VMEM((column, block, DEEP), bf),
                pltpu.VMEM((column, block, DEEP), bf),
                pltpu.VMEM((per, places, DEEP), bf),
                pltpu.VMEM((L, 8 * ((n + 7) // 8), 128), jnp.int32),
                pltpu.VMEM((L * n, RANK, WIDTH), bf),
                pltpu.VMEM((L * n, RANK, OUT), bf),
                pltpu.VMEM((3, 1024, WIDTH), bf),
                pltpu.VMEM((OUT, WIDTH), bf),
                pltpu.VMEM((per, SKIP, places), bf),
                pltpu.VMEM((per, places, SKIP), bf),
                pltpu.VMEM((places, WIDTH), bf),
                pltpu.VMEM((3, places + 2 * LAT_W, 1024), f32),
                pltpu.VMEM((per, places, OUT), f32),
                pltpu.VMEM((WIDTH, WIDTH), bf),
                dma((per, B)), dma((per, B)), dma((3, L)), dma((3, L)), dma((2, L)), dma((2, L)), dma((4,)),
                dma((18,)),
            ],
            compiler_params=pltpu.CompilerParams(
                collective_id=0, has_side_effects=True, vmem_limit_bytes=60 * 1024 * 1024),
        )(tp, req, lib, cached, down, up, skip.transpose(0, 2, 1), kw.transpose(0, 1, 3, 2), sc.T,
          gain[None], offset[None], bias[None], jnp.asarray(same_group(), bf))
        return out.transpose(0, 2, 1)

    both = P(("batch", "lib"), None, None)
    lib3 = P("lib", None, None)
    in_specs = (both, P("lib", "batch", None), P("lib", None), P(("batch", "lib")), P("lib"), lib3, lib3,
                P(), P(), P(), P(), P())
    return jax.shard_map(local, mesh=mesh, in_specs=in_specs, out_specs=both, check_vma=False)
```

time: 96.3 us -> 77.8 us (0.81)
  local copies, waits for them, and re-layouts: 20.9 us -> 3.71 us
  Pallas kernels: 75 us -> 73.9 us
    unnamed x21 -> x1, local copies, waits for them, and re-layouts: 17.1 us -> 2.47 us
    pallas_call x1 -> x0, local copies, waits for them, and re-layouts: 2.5 us -> none  [compute(): pl.pallas_call(block_kernel, grid=(per,), out_shape=jax.ShapeDtypeStruct(...]
    pallas_call x2 -> x1, Pallas kernels: 75 us -> 73.9 us  [local(): pl.pallas_call(functools.partial(kernel, B, L), out_shape=jax.ShapeDtypeS...]
where the time goes in v2:
time: 77.8 us; the launch traced here: 77.6 us
  Pallas kernels  73.9 us (95%)
  local copies, waits for them, and re-layouts  3.71 us (5%)
    pallas_call x1, Pallas kernels, local(): pl.pallas_call(functools.partial(kernel, B, L), out_shape=jax.ShapeDtypeS...  73.9 us
    unnamed x1, local copies, waits for them, and re-layouts  2.47 us

profile of v2, /device:TPU:9, one launch (start us, length us, event | category | flops | bytes accessed | tf_op | source)
XLA Modules:
  0.0 77.6 jit_solution(13338355309570800444)
XLA Ops:
  0.0 1.2 %broadcast_in_dim.11.bias = f32[1,320]{1,0:T(1,128)} reshape(f32[320]{0:T(512)} %param.24) | data formatting | bytes 2560 | tf_op jit(solution)/shard_map/broadcast_in_dim | solution.py:301
  1.2 73.9 %shard_map.127 = bf16[2,320,1024]{2,1,0:T(8,128)(2,1)} custom-call(s32[1,16]{1,0:T(1,128)} %tp.1, s32[2]{0:T(128)} %req.1, s32[4]{0:T(128)} %lib.1, bf16[16,128,640]{2,1,0:T(8,128)(2,1)} %cached_h.1, bf16[4,64,960]{2,1,0:T(8,128)(2,1)} %down.1, bf16[4,64,320]{2,1,0:T(8,128)(2,1)} %up.1, bf16[2,320,1024]{2,1,0:T(8,128)(2,1)} %bitcast.8, ...), custom_call_target="tpu_custom_call" | custom-call | tf_op jit(solution)/shard_map/pallas_call | solution.py:275
  75.2 2.5 %copy.15 = bf16[2,1024,320]{1,2,0:T(8,128)(2,1)} copy(bf16[2,1024,320]{1,2,0:T(8,128)(2,1)} %bitcast.7) | data formatting | bytes 2621440

commit v3 on v2

--- a/solution.py
+++ b/solution.py
@@ -94,18 +94,23 @@
             j = jnp.where(tp[0, i] == t, i, j)
         return j
 
-    def z_copies(z, src):
-        part = pl.ds(half * h, h)
+    def inside(v):
+        return jnp.logical_and(v >= 0, v < L)
+
+    def z_copies(way, src):
         row = pl.ds(src * n + half * h, h)
-        kw = dict(device_id=(b, z), device_id_type=MESH)
+        kw = dict(device_id=(b, (l + way + L) % L), device_id_type=MESH)
         return [
-            pltpu.make_async_remote_copy(src_ref=ids.at[src], dst_ref=ids.at[src],
-                                         send_sem=z_send.at[0, z], recv_sem=z_recv.at[0, src], **kw),
-            pltpu.make_async_remote_copy(src_ref=down.at[part], dst_ref=dall.at[row],
-                                         send_sem=z_send.at[1, z], recv_sem=z_recv.at[1, src], **kw),
-            pltpu.make_async_remote_copy(src_ref=up.at[part], dst_ref=uall.at[row],
-                                         send_sem=z_send.at[2, z], recv_sem=z_recv.at[2, src], **kw),
+            pltpu.make_async_remote_copy(src_ref=ref, dst_ref=ref, send_sem=z_send.at[i, (way + 1) // 2, src],
+                                         recv_sem=z_recv.at[i, src], **kw)
+            for i, ref in enumerate((ids.at[src], dall.at[row], uall.at[row]))
         ]
+
+    def pass_on(way, src, done=False):
+        @pl.when(inside(l + way))
+        def _():
+            for c in z_copies(way, src):
+                c.wait_send() if done else c.start()
 
     def f_copies(src, side):
         row = pl.ds(src * n + side * h, h)
@@ -117,26 +122,46 @@
                                          send_sem=f_send.at[1, src], recv_sem=f_recv.at[1, src], **kw),
         ]
 
+    def z_step(d):
+        for way in (1, -1):
+            src = l - way * d
+
+            @pl.when(inside(src))
+            def _():
+                for c in z_copies(way, src):
+                    c.wait_recv()
+                pass_on(way, src)
+                for c in f_copies(src, half):
+                    c.start()
+
+    def z_sent(d):
+        for way in (1, -1):
+            src = l - way * d
+
+            @pl.when(inside(src))
+            def _():
+                pass_on(way, src, done=True)
+
+    dall[pl.ds(l * n, n)] = down[...]
+    uall[pl.ds(l * n, n)] = up[...]
     load_cached.wait()
     for s in range(per):
         for p in peers:
             send[p * per + s] = cached[slot(p * per + s)]
-            to_peer(s, p, b).start()
+            if s == 0:
+                to_peer(s, p, b).start()
         if s == 0:
             row_id = lax.broadcasted_iota(jnp.int32, ids.shape[1:], 0)
             mine = jnp.full(ids.shape[1:], -1, jnp.int32)
             for i in range(n):
                 mine = jnp.where(row_id == i, lib[i], mine)
             ids[l] = mine
-            for z in zpeers:
-                for c in z_copies(z, l):
-                    c.start()
+            for way in (1, -1):
+                pass_on(way, l)
     for c in loads + w_loads:
         c.start()
     for s in range(per):
         deep[s, pl.ds(pl.multiple_of(b * block, block), block), :] = cached[slot(b * per + s)]
-    dall[pl.ds(l * n, n)] = down[...]
-    uall[pl.ds(l * n, n)] = up[...]
     edge = jnp.zeros((3, LAT_W, 1024), jnp.float32)
     y[:, :LAT_W, :] = edge
     y[:, places + LAT_W:, :] = edge
@@ -149,12 +174,15 @@
             sk = skip_t[s, :, at].astype(jnp.float32).T.astype(jnp.bfloat16)
             skip[s, at, :] = sk
             acc[s, at, :] = dot_t(sk, sc[:, :SKIP]) + bias[...]
-
-    for z in zpeers:
-        for c in z_copies(z, z):
-            c.wait_recv()
-        for c in f_copies(z, half):
-            c.start()
+        if s + 1 < L - 1:
+            z_step(s + 1)
+
+    for s in range(1, per):
+        for p in peers:
+            to_peer(s - 1, p, b).wait_send()
+            to_peer(s, p, b).start()
+    for d in range(min(per, L - 2) + 1, L):
+        z_step(d)
     for z in zpeers:
         for c in f_copies(z, 1 - half):
             c.wait_recv()
@@ -162,7 +190,7 @@
         c.wait()
     number = lax.broadcasted_iota(jnp.int32, ids.shape, 0) * n + lax.broadcasted_iota(jnp.int32, ids.shape, 1)
     count = places * (WIDTH // GROUPS)
-    step = 64
+    step = 256
 
     def request(s, carry):
         k = jnp.max(jnp.where(ids[...] == req[s], number, 0))
@@ -251,14 +279,13 @@
         return carry
 
     lax.fori_loop(0, per, request, 0)
+    for d in range(L):
+        z_sent(d)
     for z in zpeers:
-        for c in z_copies(z, l):
-            c.wait_send()
         for c in f_copies(z, half):
             c.wait_send()
-    for s in range(per):
-        for p in peers:
-            to_peer(s, p, b).wait_send()
+    for p in peers:
+        to_peer(per - 1, p, b).wait_send()
 
 
 def solution(mesh):
@@ -292,7 +319,7 @@
                 pltpu.VMEM((3, places + 2 * LAT_W, 1024), f32),
                 pltpu.VMEM((per, places, OUT), f32),
                 pltpu.VMEM((WIDTH, WIDTH), bf),
-                dma((per, B)), dma((per, B)), dma((3, L)), dma((3, L)), dma((2, L)), dma((2, L)), dma((4,)),
+                dma((per, B)), dma((per, B)), dma((3, 2, L)), dma((3, L)), dma((2, L)), dma((2, L)), dma((4,)),
                 dma((18,)),
             ],
             compiler_params=pltpu.CompilerParams(

time: 77.8 us -> 69 us (0.89)
  the two profiles are of different devices: /device:TPU:9 before, /device:TPU:1 now
where the time goes in v3:
time: 69 us; the launch traced here: 68.9 us
  Pallas kernels  65.1 us (94%)
  local copies, waits for them, and re-layouts  3.71 us (5%)
    pallas_call x1, Pallas kernels, local(): pl.pallas_call(functools.partial(kernel, B, L), out_shape=jax.ShapeDtypeS...  65.1 us
    unnamed x1, local copies, waits for them, and re-layouts  2.47 us

profile of v3, /device:TPU:1, one launch (start us, length us, event | category | flops | bytes accessed | tf_op | source)
XLA Modules:
  0.0 68.9 jit_solution(8796537793497865224)
XLA Ops:
  0.0 1.2 %broadcast_in_dim.11.bias = f32[1,320]{1,0:T(1,128)} reshape(f32[320]{0:T(512)} %param.24) | data formatting | bytes 2560 | tf_op jit(solution)/shard_map/broadcast_in_dim | solution.py:328
  1.2 65.1 %shard_map.127 = bf16[2,320,1024]{2,1,0:T(8,128)(2,1)} custom-call(s32[1,16]{1,0:T(1,128)} %tp.1, s32[2]{0:T(128)} %req.1, s32[4]{0:T(128)} %lib.1, bf16[16,128,640]{2,1,0:T(8,128)(2,1)} %cached_h.1, bf16[4,64,960]{2,1,0:T(8,128)(2,1)} %down.1, bf16[4,64,320]{2,1,0:T(8,128)(2,1)} %up.1, bf16[2,320,1024]{2,1,0:T(8,128)(2,1)} %bitcast.8, ...), custom_call_target="tpu_custom_call" | custom-call | tf_op jit(solution)/shard_map/pallas_call | solution.py:302
  66.4 2.5 %copy.15 = bf16[2,1024,320]{1,2,0:T(8,128)(2,1)} copy(bf16[2,1024,320]{1,2,0:T(8,128)(2,1)} %bitcast.7) | data formatting | bytes 2621440

commit v4 on v3

--- a/solution.py
+++ b/solution.py
@@ -144,20 +144,19 @@
 
     dall[pl.ds(l * n, n)] = down[...]
     uall[pl.ds(l * n, n)] = up[...]
+    row_id = lax.broadcasted_iota(jnp.int32, ids.shape[1:], 0)
+    mine = jnp.full(ids.shape[1:], -1, jnp.int32)
+    for i in range(n):
+        mine = jnp.where(row_id == i, lib[i], mine)
+    ids[l] = mine
+    for way in (1, -1):
+        pass_on(way, l)
     load_cached.wait()
     for s in range(per):
         for p in peers:
             send[p * per + s] = cached[slot(p * per + s)]
             if s == 0:
                 to_peer(s, p, b).start()
-        if s == 0:
-            row_id = lax.broadcasted_iota(jnp.int32, ids.shape[1:], 0)
-            mine = jnp.full(ids.shape[1:], -1, jnp.int32)
-            for i in range(n):
-                mine = jnp.where(row_id == i, lib[i], mine)
-            ids[l] = mine
-            for way in (1, -1):
-                pass_on(way, l)
     for c in loads + w_loads:
         c.start()
     for s in range(per):
@@ -181,11 +180,6 @@
         for p in peers:
             to_peer(s - 1, p, b).wait_send()
             to_peer(s, p, b).start()
-    for d in range(min(per, L - 2) + 1, L):
-        z_step(d)
-    for z in zpeers:
-        for c in f_copies(z, 1 - half):
-            c.wait_recv()
     for c in w_loads:
         c.wait()
     number = lax.broadcasted_iota(jnp.int32, ids.shape, 0) * n + lax.broadcasted_iota(jnp.int32, ids.shape, 1)
@@ -193,9 +187,6 @@
     step = 256
 
     def request(s, carry):
-        k = jnp.max(jnp.where(ids[...] == req[s], number, 0))
-        w[1, 3 * OUT:, :] = dall[k]
-        u = uall[k]
         for p in peers:
             to_peer(s, p, p).wait_recv()
 
@@ -237,6 +228,18 @@
             return c
 
         lax.fori_loop(0, places // step, normed, 0)
+
+        @pl.when(s == 0)
+        def _():
+            for d in range(min(per, L - 2) + 1, L):
+                z_step(d)
+            for z in zpeers:
+                for c in f_copies(z, 1 - half):
+                    c.wait_recv()
+
+        k = jnp.max(jnp.where(ids[...] == req[s], number, 0))
+        w[1, 3 * OUT:, :] = dall[k]
+        u = uall[k]
 
         def conv(i, c):
             p = pl.multiple_of(i * CHUNK, CHUNK)

time: 69 us -> 65.3 us (0.946)
  Pallas kernels: 65.1 us -> 61.4 us
    pallas_call x1, Pallas kernels: 65.1 us -> 61.4 us  [local(): pl.pallas_call(functools.partial(kernel, B, L), out_shape=jax.ShapeDtypeS...]
where the time goes in v4:
time: 65.3 us; the launch traced here: 65.1 us
  Pallas kernels  61.4 us (94%)
  local copies, waits for them, and re-layouts  3.71 us (6%)
    pallas_call x1, Pallas kernels, local(): pl.pallas_call(functools.partial(kernel, B, L), out_shape=jax.ShapeDtypeS...  61.4 us
    unnamed x1, local copies, waits for them, and re-layouts  2.47 us

profile of v4, /device:TPU:1, one launch (start us, length us, event | category | flops | bytes accessed | tf_op | source)
XLA Modules:
  0.0 65.1 jit_solution(3259551054839904168)
XLA Ops:
  0.0 1.2 %broadcast_in_dim.11.bias = f32[1,320]{1,0:T(1,128)} reshape(f32[320]{0:T(512)} %param.24) | data formatting | bytes 2560 | tf_op jit(solution)/shard_map/broadcast_in_dim | solution.py:331
  1.2 61.4 %shard_map.127 = bf16[2,320,1024]{2,1,0:T(8,128)(2,1)} custom-call(s32[1,16]{1,0:T(1,128)} %tp.1, s32[2]{0:T(128)} %req.1, s32[4]{0:T(128)} %lib.1, bf16[16,128,640]{2,1,0:T(8,128)(2,1)} %cached_h.1, bf16[4,64,960]{2,1,0:T(8,128)(2,1)} %down.1, bf16[4,64,320]{2,1,0:T(8,128)(2,1)} %up.1, bf16[2,320,1024]{2,1,0:T(8,128)(2,1)} %bitcast.8, ...), custom_call_target="tpu_custom_call" | custom-call | tf_op jit(solution)/shard_map/pallas_call | solution.py:305
  62.6 2.5 %copy.15 = bf16[2,1024,320]{1,2,0:T(8,128)(2,1)} copy(bf16[2,1024,320]{1,2,0:T(8,128)(2,1)} %bitcast.7) | data formatting | bytes 2621440
